TPU v7x, 32 devices: a whole 2x2x4 slice. The times are simulated.
32 devices in a mesh: groups: 2 (over y), wide: 4 (over z), loop: 4 (over x, core).
Axes of the slice: x: 2, y: 2, z: 4, core: 2. Of those that a mesh axis runs over, the one named last changes fastest.
Arguments:
- image_embed: bfloat16 [2048, 1152], P(('groups', 'wide', 'loop')), parts along dimension 0, may hold values from -24 to 24
- text_embed: bfloat16 [2048, 1152], P(('groups', 'wide', 'loop')), parts along dimension 0, may hold values from -24 to 24
- pair_index: int32 [2048], P(('groups', 'wide', 'loop')), parts along dimension 0, may hold values from 0 to 1023, as said below
- logit_scale: float32 [1], replicated, may hold values from 5 to 15
- logit_bias: float32 [1], replicated, may hold values from -3 to -1
Outputs:
- text_grad: float32 [2048, 1152], P(('groups', 'wide', 'loop')), parts along dimension 0
- mean_loss: float32 [2], P('groups'), parts along dimension 0
There are 2 independent parts, one for each index of `groups`. A program takes and returns all parts, laid end to end along the dimension named above; an argument that names none is the same for every part. Nothing has to cross between parts.
Inputs may be any that keep to these rules, and one draw needn't show every extreme that they name: A permutation of 0 to 1023: image i is paired with text pair_index[i].
All inputs are finite; a program needn't handle non-finite values.
Results may differ from a plain program's by a relative error of at most 0.00049.
Values may be sent and summed in bfloat16 or wider, within the bound.
A program may use at most 64 MiB of HBM per device.

v0:
```python
import jax
import jax.numpy as jnp
from jax import lax
from jax.sharding import PartitionSpec as P

epsilon = 1e-06


def passed_along(block, axis, distance):
    devices = range(lax.axis_size(axis))
    route = [((i - distance) % len(devices), i) for i in devices]
    return lax.ppermute(block, axis, route)


def normalize(values):
    wide_values = values.astype(jnp.float32)
    inverse = lax.rsqrt(jnp.sum(wide_values * wide_values, axis=1, keepdims=True) + epsilon)
    return (wide_values * inverse, inverse)


def pair_terms(text_block, first_row, image_bf, pairs, scale_value, bias_value):
    scores = lax.dot_general(
        text_block, image_bf, (((1,), (1,)), ((), ())), preferred_element_type=jnp.float32
    )
    logits = scale_value * scores + bias_value
    columns = first_row + lax.broadcasted_iota(jnp.int32, (text_block.shape[0], 1), 0)
    positive = pairs[None, :] == columns
    signed = jnp.where(positive, logits, -logits)
    loss_part = -jnp.sum(jax.nn.log_sigmoid(signed))
    weights = (scale_value * (jax.nn.sigmoid(logits) - positive.astype(jnp.float32))).astype(
        jnp.bfloat16
    )
    partial_sum = jnp.dot(weights, image_bf, preferred_element_type=jnp.float32)
    return (loss_part, partial_sum)


def shards(image_embed, text_embed, pair_index, logit_scale, logit_bias):
    local_rows = text_embed.shape[0]
    width_dim = text_embed.shape[1]
    loop_size = lax.axis_size("loop")
    loop_index = lax.axis_index("loop")
    wide_index = lax.axis_index("wide")
    scale_value = logit_scale[0]
    bias_value = logit_bias[0]
    image_unit, _ = normalize(image_embed)
    image_bf = image_unit.astype(jnp.bfloat16)
    text_hat, inverse = normalize(text_embed)
    text_bf = text_hat.astype(jnp.bfloat16)
    group_first = wide_index * loop_size * local_rows
    gathered, gathered_pairs = (
        lax.all_gather(image_bf, "wide", axis=0, tiled=True),
        lax.all_gather(pair_index, "wide", axis=0, tiled=True),
    )
    loss_sum = jnp.zeros((), jnp.float32)
    text_block = text_bf
    accumulated = jnp.zeros((local_rows, width_dim), jnp.float32)
    for cycle_step in range(loop_size):
        owner_block = (loop_index - cycle_step) % loop_size
        first_row = group_first + owner_block * local_rows
        loss_part, partial_sum = pair_terms(
            text_block, first_row, gathered, gathered_pairs, scale_value, bias_value
        )
        loss_sum = loss_sum + loss_part
        accumulated = accumulated + partial_sum
        if cycle_step + 1 < loop_size:
            text_block = passed_along(text_block, "loop", 1)
            accumulated = passed_along(accumulated, "loop", 1)
    unit_grad = passed_along(accumulated, "loop", 1)
    along = jnp.sum(text_hat * unit_grad, axis=1, keepdims=True)
    text_grad = (unit_grad - text_hat * along) * inverse
    pairs_total = float(local_rows * lax.axis_size("wide") * loop_size)
    total_loss = lax.psum(loss_sum, ("wide", "loop"))
    mean_loss = jnp.reshape(total_loss / (pairs_total * pairs_total), (1,))
    return (text_grad, mean_loss)


def solution(mesh):
    return jax.shard_map(
        shards,
        mesh=mesh,
        in_specs=(
            P(("groups", "wide", "loop"), None),
            P(("groups", "wide", "loop"), None),
            P(("groups", "wide", "loop")),
            P(),
            P(),
        ),
        out_specs=(P(("groups", "wide", "loop"), None), P("groups")),
        check_vma=False,
    )
```

profile of v0, /device:TPU:0, one launch (start us, length us, event | category | flops | bytes accessed | tf_op | source)
XLA Modules:
  0.0 91.3 jit_solution(12978916182630606298)
XLA Ops:
  0.6 0.0 copy-start
  0.6 1.1 %fusion.10 = f32[64]{0:T(128)S(1)} fusion(bf16[64,1152]{1,0:T(8,128)(2,1)} %param.6), kind=kLoop, calls=%fused_computation.19 | loop fusion | flops 221120 | bytes 147712 | tf_op jit(solution)/shard_map/reduce_sum | solution.py:17
  1.8 0.0 copy-done
  1.8 0.0 copy-start.1
  1.8 0.1 fusion.6
  1.9 0.5 collective-permute-start.1
  2.4 0.3 copy-done.1
  2.7 0.1 fusion.11
  2.8 0.1 fusion.12
  2.9 19.1 %all_gather.6 = bf16[256,1152]{1,0:T(8,128)(2,1)S(1)} all-gather(bf16[64,1152]{1,0:T(8,128)(2,1)S(1)} %fusion.12), channel_id=1, replica_groups=mesh['groups'=2,'wide'=4,'loop'=4] {'wide'}, dimensions={0}, use_global_device_ids=true | all-gather | bytes 737280 | tf_op jit(solution)/shard_map/all_gather | solution.py:51
  23.3 0.0 copy-start.3
  23.3 0.6 copy-done.3
  24.0 0.7 dynamic-slice
  25.3 0.0 copy-start.2
  25.4 0.6 copy-done.2
  26.0 0.2 dynamic-update-slice
  26.2 7.2 %all-reduce = s32[256]{0:T(256)S(1)} all-reduce(s32[256]{0:T(256)S(1)} %dynamic-update-slice), channel_id=1, replica_groups=mesh['groups'=2,'wide'=4,'loop'=4] {'wide'}, use_global_device_ids=true, to_apply=%add | all-reduce | flops 256 | bytes 2048
  33.4 0.3 fusion.3
  33.7 0.3 fusion.46
  34.0 0.1 collective-permute-start
  34.2 0.0 collective-permute-done.1
  34.2 1.4 %collective-permute-start.3 = (bf16[64,1152]{1,0:T(8,128)(2,1)S(1)}, bf16[64,1152]{1,0:T(8,128)(2,1)S(1)}, u32[]{:S(2)}, u32[]{:S(2)}) collective-permute-start(bf16[64,1152]{1,0:T(8,128)(2,1)S(1)} %collective-permute-done.1), channel_id=1, source_target_pairs={{3,0},{0,1},{1,2},{2,3},{7,4},{4,5},{5,6},{6,7},{11,8},{8,9},{9,10... | collective-permute-start | bytes 442376 | tf_op jit(solution)/shard_map/ppermute | solution.py:12
  35.5 0.3 fusion.2
  35.9 4.3 %collective-permute-done = f32[64,1152]{1,0:T(8,128)S(1)} collective-permute-done((f32[64,1152]{1,0:T(8,128)S(1)}, f32[64,1152]{1,0:T(8,128)S(1)}, u32[]{:S(2)}, u32[]{:S(2)}) %collective-permute-start) | collective-permute-done | bytes 294944 | tf_op jit(solution)/shard_map/ppermute | solution.py:12
  40.2 0.3 convolution_add_fusion
  40.5 0.1 collective-permute-start.2
  40.5 1.3 %collective-permute-done.3 = bf16[64,1152]{1,0:T(8,128)(2,1)S(1)} collective-permute-done((bf16[64,1152]{1,0:T(8,128)(2,1)S(1)}, bf16[64,1152]{1,0:T(8,128)(2,1)S(1)}, u32[]{:S(2)}, u32[]{:S(2)}) %collective-permute-start.3) | collective-permute-done | bytes 147488 | tf_op jit(solution)/shard_map/ppermute | solution.py:12
  41.8 0.1 collective-permute-start.5
  41.9 0.3 fusion.1
  42.3 0.3 fusion.43
  42.5 4.2 %collective-permute-done.2 = f32[64,1152]{1,0:T(8,128)S(1)} collective-permute-done((f32[64,1152]{1,0:T(8,128)S(1)}, f32[64,1152]{1,0:T(8,128)S(1)}, u32[]{:S(2)}, u32[]{:S(2)}) %collective-permute-start.2) | collective-permute-done | bytes 294944 | tf_op jit(solution)/shard_map/ppermute | solution.py:12
  46.7 0.1 collective-permute-start.4
  46.8 1.5 %collective-permute-done.5 = bf16[64,1152]{1,0:T(8,128)(2,1)S(1)} collective-permute-done((bf16[64,1152]{1,0:T(8,128)(2,1)S(1)}, bf16[64,1152]{1,0:T(8,128)(2,1)S(1)}, u32[]{:S(2)}, u32[]{:S(2)}) %collective-permute-start.5) | collective-permute-done | bytes 147488 | tf_op jit(solution)/shard_map/ppermute | solution.py:12
  48.2 1.1 %fusion.40 = (f32[]{:T(128)}, f32[]{:T(128)}, f32[]{:T(128)}, f32[]{:T(128)}, f32[64,256]{1,0:T(8,128)S(1)}) fusion(s32[256]{0:T(256)S(1)} %all-reduce, s32[64]{0:T(128)S(1)} %iota_add_fusion, f32[64,256]{1,0:T(8,128)S(1)} %fusion.1, s32[64]{0:T(128)S(1)} %iota_add_fusion.1, f32[64,256]{1,0:T(8,128)S(1)} %fusion.2, s32[64]{0:T(128)S(1)} %iota_add_fusion.2, ...), kind=kOutput, calls=%fused_computation.65 | convolution fusion | flops 38502400 | bytes 1001496 | tf_op jit(solution)/shard_map/dot_general | solution.py:22
  49.3 0.3 fusion.41
  49.6 3.3 %collective-permute-done.4 = f32[64,1152]{1,0:T(8,128)S(1)} collective-permute-done((f32[64,1152]{1,0:T(8,128)S(1)}, f32[64,1152]{1,0:T(8,128)S(1)}, u32[]{:S(2)}, u32[]{:S(2)}) %collective-permute-start.4) | collective-permute-done | bytes 294944 | tf_op jit(solution)/shard_map/ppermute | solution.py:12
  52.9 0.1 collective-permute-start.6
  55.5 33.0 %psum.7 = f32[]{:T(128)} all-reduce(f32[]{:T(128)S(6)} %add.188), channel_id=1, replica_groups=mesh['groups'=2,'wide'=4,'loop'=4] {'wide','loop'}, use_global_device_ids=true, to_apply=%region_7.8 | all-reduce | flops 1 | bytes 8 | tf_op jit(solution)/shard_map/psum | solution.py:72
  89.1 0.0 collective-permute-done.6
  89.2 0.2 fusion.7
  89.4 0.8 fusion.9
  (9 shorter events, 0.1 us)
Async XLA Ops:
  0.6 1.1 %copy-start = (bf16[64,1152]{1,0:T(8,128)(2,1)S(1)}, bf16[64,1152]{1,0:T(8,128)(2,1)}, u32[]{:S(2)}) copy-start(bf16[64,1152]{1,0:T(8,128)(2,1)} %param.6) | copy-start | bytes 442372
  1.8 0.9 %copy-start.1 = (bf16[64,1152]{1,0:T(8,128)(2,1)S(1)}, bf16[64,1152]{1,0:T(8,128)(2,1)}, u32[]{:S(2)}) copy-start(bf16[64,1152]{1,0:T(8,128)(2,1)} %param.5) | copy-start | bytes 442372
  1.9 32.3 %collective-permute-start.1 = (bf16[64,1152]{1,0:T(8,128)(2,1)S(1)}, bf16[64,1152]{1,0:T(8,128)(2,1)S(1)}, u32[]{:S(2)}, u32[]{:S(2)}) collective-permute-start(bf16[64,1152]{1,0:T(8,128)(2,1)S(1)} %fusion.6), channel_id=1, source_target_pairs={{3,0},{0,1},{1,2},{2,3},{7,4},{4,5},{5,6},{6,7},{11,8},{8,9},{9,10... | collective-permute-start | bytes 442376 | tf_op jit(solution)/shard_map/ppermute | solution.py:12
  23.3 0.7 copy-start.3
  25.3 0.7 copy-start.2
  34.0 6.2 %collective-permute-start = (f32[64,1152]{1,0:T(8,128)S(1)}, f32[64,1152]{1,0:T(8,128)S(1)}, u32[]{:S(2)}, u32[]{:S(2)}) collective-permute-start(f32[64,1152]{1,0:T(8,128)S(1)} %fusion.46), channel_id=1, source_target_pairs={{3,0},{0,1},{1,2},{2,3},{7,4},{4,5},{5,6},{6,7},{11,8},{8,9},{9,10... | collective-permute-start | bytes 884744 | tf_op jit(solution)/shard_map/ppermute | solution.py:12
  34.2 7.6 %collective-permute-start.3 = (bf16[64,1152]{1,0:T(8,128)(2,1)S(1)}, bf16[64,1152]{1,0:T(8,128)(2,1)S(1)}, u32[]{:S(2)}, u32[]{:S(2)}) collective-permute-start(bf16[64,1152]{1,0:T(8,128)(2,1)S(1)} %collective-permute-done.1), channel_id=1, source_target_pairs={{3,0},{0,1},{1,2},{2,3},{7,4},{4,5},{5,6},{6,7},{11,8},{8,9},{9,10... | collective-permute-start | bytes 442376 | tf_op jit(solution)/shard_map/ppermute | solution.py:12
  40.5 6.2 %collective-permute-start.2 = (f32[64,1152]{1,0:T(8,128)S(1)}, f32[64,1152]{1,0:T(8,128)S(1)}, u32[]{:S(2)}, u32[]{:S(2)}) collective-permute-start(f32[64,1152]{1,0:T(8,128)S(1)} %convolution_add_fusion), channel_id=1, source_target_pairs={{3,0},{0,1},{1,2},{2,3},{7,4},{4,5},{5,6},{6,7},{11,8},{8,9},{9,10... | collective-permute-start | bytes 884744 | tf_op jit(solution)/shard_map/ppermute | solution.py:12
  41.8 6.5 %collective-permute-start.5 = (bf16[64,1152]{1,0:T(8,128)(2,1)S(1)}, bf16[64,1152]{1,0:T(8,128)(2,1)S(1)}, u32[]{:S(2)}, u32[]{:S(2)}) collective-permute-start(bf16[64,1152]{1,0:T(8,128)(2,1)S(1)} %collective-permute-done.3), channel_id=1, source_target_pairs={{3,0},{0,1},{1,2},{2,3},{7,4},{4,5},{5,6},{6,7},{11,8},{8,9},{9,10... | collective-permute-start | bytes 442376 | tf_op jit(solution)/shard_map/ppermute | solution.py:12
  46.7 6.2 %collective-permute-start.4 = (f32[64,1152]{1,0:T(8,128)S(1)}, f32[64,1152]{1,0:T(8,128)S(1)}, u32[]{:S(2)}, u32[]{:S(2)}) collective-permute-start(f32[64,1152]{1,0:T(8,128)S(1)} %add.174), channel_id=1, source_target_pairs={{3,0},{0,1},{1,2},{2,3},{7,4},{4,5},{5,6},{6,7},{11,8},{8,9},{9,10... | collective-permute-start | bytes 884744 | tf_op jit(solution)/shard_map/ppermute | solution.py:12
  52.9 36.2 %collective-permute-start.6 = (f32[64,1152]{1,0:T(8,128)S(1)}, f32[64,1152]{1,0:T(8,128)S(1)}, u32[]{:S(2)}, u32[]{:S(2)}) collective-permute-start(f32[64,1152]{1,0:T(8,128)S(1)} %add.181), channel_id=1, source_target_pairs={{3,0},{0,1},{1,2},{2,3},{7,4},{4,5},{5,6},{6,7},{11,8},{8,9},{9,10... | collective-permute-start | bytes 884744 | tf_op jit(solution)/shard_map/ppermute | solution.py:12
where the time goes:
time: 91.6 us; the launch traced here: 91.3 us
  blocking collectives  59.3 us (65%)
  waiting for transfers between devices  14.6 us (16%)
  between operations  7.18 us (8%)
  matrix products  3.03 us (3%)
  other arithmetic  2.56 us (3%)
  local copies, waits for them, and re-layouts  2.44 us (3%)
  starting transfers between devices  2.23 us (2%)
    psum x1, blocking collectives, shards(): total_loss = lax.psum(loss_sum, ('wide', 'loop'))  33 us
    all_gather x1, blocking collectives, shards(): lax.all_gather(image_bf, 'wide', axis=0, tiled=True)  19.1 us
    ppermute x7, waiting for transfers between devices, passed_along(): return lax.ppermute(block, axis, route)  14.6 us
    unnamed x1, blocking collectives  7.24 us
    unnamed x11, local copies, waits for them, and re-layouts  2.44 us
    ppermute x7, starting transfers between devices, passed_along(): return lax.ppermute(block, axis, route)  2.23 us
    dot_general x4, matrix products, pair_terms(): lax.dot_general(text_block, image_bf, (((1,), (1,)), ((), ())), preferred...  1.99 us
  transfers between devices with their start and end apart: 7, of which 5 were waited for; matrix products, arithmetic and copies ran while one was open for 5% of the time, Pallas kernels for 0%

commit v1 on v0

--- a/solution.py
+++ b/solution.py
@@ -1,9 +1,14 @@
+import functools
+
 import jax
 import jax.numpy as jnp
 from jax import lax
+from jax.experimental import pallas as pl
+from jax.experimental.pallas import tpu as pltpu
 from jax.sharding import PartitionSpec as P
 
 epsilon = 1e-06
+MESH = pl.DeviceIdType.MESH
 
 
 def passed_along(block, axis, distance):
@@ -34,7 +39,7 @@
     return (loss_part, partial_sum)
 
 
-def shards(image_embed, text_embed, pair_index, logit_scale, logit_bias):
+def ring_shards(image_embed, text_embed, pair_index, logit_scale, logit_bias):
     local_rows = text_embed.shape[0]
     width_dim = text_embed.shape[1]
     loop_size = lax.axis_size("loop")
@@ -74,9 +79,257 @@
     return (text_grad, mean_loss)
 
 
+def gather_kernel(
+    rows,
+    image_ref,
+    text_ref,
+    pair_ref,
+    scale_ref,
+    bias_ref,
+    grad_ref,
+    loss_ref,
+    gathered,
+    pair_all,
+    pair_rows,
+    loss_all,
+    loss_mine,
+    text_bf,
+    total,
+    send_sem,
+    recv_sem,
+    small_send,
+    small_recv,
+):
+    wide, loop = lax.axis_index("wide"), lax.axis_index("loop")
+    me = wide * 4 + loop
+    sibling = loop + 1 - 2 * (loop % 2)
+    across = (loop + 2) % 4
+    across_sibling = (sibling + 2) % 4
+    interior = (wide % 3) != 0
+    ends = (wide % 3) == 0
+    high = wide // 2
+    source = [wide, wide + 1 - 2 * (wide % 2), 2 - high, 3 - 3 * high]
+    middle = 3 - wide
+    outer = (wide - 1) * 3
+
+    barrier = pltpu.get_barrier_semaphore()
+
+    def peer(step):
+        other = (me + step) % 16
+        return {"wide": other // 4, "loop": other % 4}
+
+    for step in range(1, 16):
+        pl.semaphore_signal(barrier, inc=1, device_id=peer(step), device_id_type=MESH)
+
+    def block(place, column):
+        slot = place * 4 + column
+        return slot, gathered.at[pl.ds(pl.multiple_of(slot * rows, rows), rows), :]
+
+    image = image_ref[...].astype(jnp.float32)
+    image_inverse = lax.rsqrt(jnp.sum(image * image, axis=1, keepdims=True) + epsilon)
+    gathered[pl.ds(pl.multiple_of(me * rows, rows), rows), :] = (image * image_inverse).astype(
+        jnp.bfloat16
+    )
+    own_pairs = jnp.concatenate([pair_ref[...], jnp.zeros((1, 128 - rows), jnp.int32)], axis=1)
+    pair_all[me] = own_pairs
+    pl.semaphore_wait(barrier, 15)
+
+    def send(number, place, column, to):
+        slot, view = block(place, column)
+        copy = pltpu.make_async_remote_copy(
+            src_ref=view,
+            dst_ref=view,
+            send_sem=send_sem.at[number],
+            recv_sem=recv_sem.at[slot],
+            device_id=to,
+            device_id_type=MESH,
+        )
+        copy.start()
+
+    def sent(number):
+        view = gathered.at[pl.ds(0, rows), :]
+        pltpu.make_async_copy(view, view, send_sem.at[number]).wait()
+
+    def arrived(place, column):
+        slot, view = block(place, column)
+        pltpu.make_async_copy(view, view, recv_sem.at[slot]).wait()
+
+    send(0, wide, loop, {"wide": source[1], "loop": loop})
+
+    @pl.when(interior)
+    def _():
+        send(1, wide, loop, {"wide": middle, "loop": loop})
+
+    send(2, wide, loop, {"wide": wide, "loop": across})
+    send(3, wide, loop, {"wide": wide, "loop": sibling})
+    for step in range(1, 16):
+        pltpu.make_async_remote_copy(
+            src_ref=pair_all.at[me],
+            dst_ref=pair_all.at[me],
+            send_sem=small_send.at[0],
+            recv_sem=small_recv.at[0],
+            device_id=peer(step),
+            device_id_type=MESH,
+        ).start()
+
+    text = text_ref[...].astype(jnp.float32)
+    inverse = lax.rsqrt(jnp.sum(text * text, axis=1, keepdims=True) + epsilon)
+    text_bf[...] = (text * inverse).astype(jnp.bfloat16)
+    scale_value = scale_ref[0]
+    bias_value = bias_ref[0]
+    fifteen = pair_all.at[pl.ds(0, 15)]
+    pltpu.make_async_copy(fifteen, fifteen, small_recv.at[0]).wait()
+    for place in range(4):
+        pair_rows[place : place + 1, :] = jnp.concatenate(
+            [pair_all[place * 4 + column][:, :rows] for column in range(4)], axis=1
+        )
+
+    def pass_on(k):
+        arrived(source[k], loop)
+
+        @pl.when(interior)
+        def _():
+            send(4 + k, source[k], loop, {"wide": middle if k == 1 else outer, "loop": loop})
+
+        send(8 + k, source[k], loop, {"wide": wide, "loop": across})
+        send(12 + k, source[k], loop, {"wide": wide, "loop": sibling})
+
+    def pass_across(k):
+        arrived(source[k], across)
+        send(16 + k, source[k], across, {"wide": wide, "loop": sibling})
+        arrived(source[k], sibling)
+        arrived(source[k], across_sibling)
+
+    columns = me * rows + lax.broadcasted_iota(jnp.int32, (rows, 4 * rows), 0)
+
+    def terms(k):
+        place = source[k]
+        images = gathered[pl.ds(pl.multiple_of(place * 4 * rows, 4 * rows), 4 * rows), :]
+        scores = lax.dot_general(
+            text_bf[...], images, (((1,), (1,)), ((), ())), preferred_element_type=jnp.float32
+        )
+        logits = scale_value * scores + bias_value
+        positive = pair_rows[pl.ds(place, 1), :] == columns
+        small = jnp.exp(-jnp.abs(logits))
+        above = 1.0 + small
+        log_above = jnp.where(above == 1.0, small, jnp.log(above) * small / jnp.where(above == 1.0, 1.0, above - 1.0))
+        loss = log_above + jnp.maximum(jnp.where(positive, -logits, logits), 0.0)
+        sigmoid = jnp.where(logits >= 0.0, 1.0, small) / above
+        weights = (scale_value * (sigmoid - jnp.where(positive, 1.0, 0.0))).astype(jnp.bfloat16)
+        tile = loss[:, :128] + loss[:, 128:]
+        tile = jnp.sum(tile.reshape(rows // 8, 8, 128), axis=0)
+        return tile, weights, images
+
+    def accumulate(k, weights, images):
+        partial = jnp.dot(weights, images, preferred_element_type=jnp.float32)
+        if k == 0:
+            total[...] = partial
+        else:
+            total[...] += partial
+
+    pass_on(1)
+
+    @pl.when(interior)
+    def _():
+        pass_on(2)
+
+    pass_across(0)
+    tile, weights, images = terms(0)
+    accumulate(0, weights, images)
+    loss_tile = tile
+
+    @pl.when(ends)
+    def _():
+        pass_on(2)
+
+    @pl.when(interior)
+    def _():
+        pass_on(3)
+
+    pass_across(1)
+    tile, weights, images = terms(1)
+    accumulate(1, weights, images)
+    loss_tile += tile
+
+    @pl.when(ends)
+    def _():
+        pass_on(3)
+
+    pass_across(2)
+    tile, weights, images = terms(2)
+    accumulate(2, weights, images)
+    loss_tile += tile
+
+    pass_across(3)
+    tile, weights, images = terms(3)
+    loss_tile += tile
+    loss_mine[...] = loss_tile
+    for step in range(1, 16):
+        pltpu.make_async_remote_copy(
+            src_ref=loss_mine,
+            dst_ref=loss_all.at[step - 1],
+            send_sem=small_send.at[1],
+            recv_sem=small_recv.at[1],
+            device_id=peer(step),
+            device_id_type=MESH,
+        ).start()
+    unit_grad = total[...] + jnp.dot(weights, images, preferred_element_type=jnp.float32)
+    text = text_ref[...].astype(jnp.float32)
+    inverse = lax.rsqrt(jnp.sum(text * text, axis=1, keepdims=True) + epsilon)
+    text_hat = text * inverse
+    along = jnp.sum(text_hat * unit_grad, axis=1, keepdims=True)
+    grad_ref[...] = (unit_grad - text_hat * along) * inverse
+
+    for number in (0, 2, 3, 9, 10, 11, 13, 14, 15, 16, 17, 18, 19):
+        sent(number)
+
+    @pl.when(interior)
+    def _():
+        for number in (1, 5, 6, 7):
+            sent(number)
+
+    pltpu.make_async_copy(fifteen, fifteen, small_send.at[0]).wait()
+    pltpu.make_async_copy(loss_all, loss_all, small_send.at[1]).wait()
+    pltpu.make_async_copy(loss_all, loss_all, small_recv.at[1]).wait()
+    whole = loss_mine[...] + jnp.sum(loss_all[...], axis=0)
+    loss_ref[0] = jnp.sum(whole) * (1.0 / float((16 * rows) ** 2))
+
+
+def gather_shards(image_embed, text_embed, pair_index, logit_scale, logit_bias):
+    rows, width = text_embed.shape
+    vmem = pl.BlockSpec(memory_space=pltpu.VMEM)
+    smem = pl.BlockSpec(memory_space=pltpu.SMEM)
+    return pl.pallas_call(
+        functools.partial(gather_kernel, rows),
+        out_shape=(
+            jax.ShapeDtypeStruct((rows, width), jnp.float32),
+            jax.ShapeDtypeStruct((1,), jnp.float32),
+        ),
+        in_specs=[vmem, vmem, vmem, smem, smem],
+        out_specs=(vmem, smem),
+        scratch_shapes=[
+            pltpu.VMEM((16 * rows, width), jnp.bfloat16),
+            pltpu.VMEM((16, 1, 128), jnp.int32),
+            pltpu.VMEM((8, 4 * rows), jnp.int32),
+            pltpu.VMEM((15, 8, 128), jnp.float32),
+            pltpu.VMEM((8, 128), jnp.float32),
+            pltpu.VMEM((rows, width), jnp.bfloat16),
+            pltpu.VMEM((rows, width), jnp.float32),
+            pltpu.SemaphoreType.DMA((20,)),
+            pltpu.SemaphoreType.DMA((16,)),
+            pltpu.SemaphoreType.DMA((2,)),
+            pltpu.SemaphoreType.DMA((2,)),
+        ],
+        compiler_params=pltpu.CompilerParams(
+            collective_id=0, has_side_effects=True, vmem_limit_bytes=32 * 1024 * 1024
+        ),
+    )(image_embed, text_embed, pair_index.reshape(1, rows), logit_scale, logit_bias)
+
+
 def solution(mesh):
+    small = mesh.shape["wide"] == 4 and mesh.shape["loop"] == 4
     return jax.shard_map(
-        shards,
+        gather_shards if small else ring_shards,
         mesh=mesh,
         in_specs=(
             P(("groups", "wide", "loop"), None),

time: 91.6 us -> 38.2 us (0.42)
  blocking collectives: 59.3 us -> 0 us
  Pallas kernels: 0 us -> 31.2 us
  waiting for transfers between devices: 14.6 us -> 0 us
  between operations: 7.18 us -> 3.68 us
  matrix products: 3.03 us -> 0 us
  other arithmetic: 2.56 us -> 0 us
  starting transfers between devices: 2.23 us -> 0 us
    psum x1 -> x0, blocking collectives: 33 us -> none  [shards(): total_loss = lax.psum(loss_sum, ('wide', 'loop'))]
    pallas_call x0 -> x1, Pallas kernels: none -> 31.2 us  [gather_shards(): pl.pallas_call(functools.partial(gather_kernel, rows), out_shape=(jax.Sha...]
    all_gather x1 -> x0, blocking collectives: 19.1 us -> none  [shards(): lax.all_gather(image_bf, 'wide', axis=0, tiled=True)]
    ppermute x7 -> x0, waiting for transfers between devices: 14.6 us -> none  [passed_along(): return lax.ppermute(block, axis, route)]
    unnamed x1 -> x0, blocking collectives: 7.24 us -> none
    dot_general x8 -> x0, matrix products: 3.03 us -> none  [the longest x4 1.99 us: pair_terms(): lax.dot_general(text_block, image_bf, (((1,), (1,)), ((), ())), preferred...]
    ppermute x7 -> x0, starting transfers between devices: 2.23 us -> none  [passed_along(): return lax.ppermute(block, axis, route)]
    reduce_sum x3 -> x0, other arithmetic: 1.44 us -> none  [the longest x2 1.23 us: normalize(): jnp.sum(wide_values * wide_values, axis=1, keepdims=True) + epsilon]
  transfers between devices with their start and end apart: 7 -> 0, of which waited for: 5 -> 0; matrix products, arithmetic and copies ran while one was open for 5% -> 0% of each run, Pallas kernels for 0% -> 0%
where the time goes in v1:
time: 38.2 us; the launch traced here: 38 us
  Pallas kernels  31.2 us (82%)
  between operations  3.68 us (10%)
  local copies, waits for them, and re-layouts  3.18 us (8%)
    pallas_call x1, Pallas kernels, gather_shards(): pl.pallas_call(functools.partial(gather_kernel, rows), out_shape=(jax.Sha...  31.2 us
    unnamed x7, local copies, waits for them, and re-layouts  3.18 us

profile of v1, /device:TPU:0, one launch (start us, length us, event | category | flops | bytes accessed | tf_op | source)
XLA Modules:
  0.0 38.0 jit_solution(5037163931990706949)
XLA Ops:
  1.9 0.0 copy-start.2
  1.9 0.6 %copy-done.2 = s32[64]{0:T(128)S(1)} copy-done((s32[64]{0:T(128)S(1)}, s32[64]{0:T(128)}, u32[]{:S(2)}) %copy-start.2) | copy-done | bytes 280
  2.6 0.0 copy-start
  2.6 0.9 %copy-done = bf16[64,1152]{1,0:T(8,128)(2,1)S(1)} copy-done((bf16[64,1152]{1,0:T(8,128)(2,1)S(1)}, bf16[64,1152]{1,0:T(8,128)(2,1)}, u32[]{:S(2)}) %copy-start) | copy-done | bytes 147480
  3.5 0.0 copy-start.1
  3.5 0.9 %copy-done.1 = bf16[64,1152]{1,0:T(8,128)(2,1)S(1)} copy-done((bf16[64,1152]{1,0:T(8,128)(2,1)S(1)}, bf16[64,1152]{1,0:T(8,128)(2,1)}, u32[]{:S(2)}) %copy-start.1) | copy-done | bytes 147480
  4.4 31.2 %shard_map.68 = (f32[64,1152]{1,0:T(8,128)S(1)}, f32[1]{0:T(128)}) custom-call(bf16[64,1152]{1,0:T(8,128)(2,1)S(1)} %copy-done, bf16[64,1152]{1,0:T(8,128)(2,1)S(1)} %copy-done.1, s32[1,64]{1,0:T(1,128)S(1)} %bitcast.1, f32[1]{0:T(128)S(6)} %copy.9.scale_ref, f32[1]{0:T(128)S(6)} %copy.10.bias_ref), custom_call_target="tpu_custom_call" | custom-call | tf_op jit(solution)/shard_map/pallas_call | solution.py:302
  35.6 0.7 %copy.11 = f32[64,1152]{1,0:T(8,128)} copy(f32[64,1152]{1,0:T(8,128)S(1)} %get-tuple-element.4) | data formatting | bytes 589824
Async XLA Ops:
  1.9 0.7 %copy-start.2 = (s32[64]{0:T(128)S(1)}, s32[64]{0:T(128)}, u32[]{:S(2)}) copy-start(s32[64]{0:T(128)} %param.7) | copy-start | bytes 772
  2.6 0.9 %copy-start = (bf16[64,1152]{1,0:T(8,128)(2,1)S(1)}, bf16[64,1152]{1,0:T(8,128)(2,1)}, u32[]{:S(2)}) copy-start(bf16[64,1152]{1,0:T(8,128)(2,1)} %image_ref.1) | copy-start | bytes 442372
  3.5 0.9 %copy-start.1 = (bf16[64,1152]{1,0:T(8,128)(2,1)S(1)}, bf16[64,1152]{1,0:T(8,128)(2,1)}, u32[]{:S(2)}) copy-start(bf16[64,1152]{1,0:T(8,128)(2,1)} %text_ref.1) | copy-start | bytes 442372

commit v2 on v1

--- a/solution.py
+++ b/solution.py
@@ -79,22 +79,29 @@
     return (text_grad, mean_loss)
 
 
+PARTS = 2
+
+
 def gather_kernel(
     rows,
-    image_ref,
-    text_ref,
-    pair_ref,
+    image_hbm,
+    text_hbm,
+    pair_hbm,
     scale_ref,
     bias_ref,
     grad_ref,
     loss_ref,
     gathered,
+    image_raw,
+    text_raw,
+    pair_raw,
     pair_all,
     pair_rows,
     loss_all,
     loss_mine,
     text_bf,
     total,
+    load_sem,
     send_sem,
     recv_sem,
     small_send,
@@ -111,6 +118,15 @@
     source = [wide, wide + 1 - 2 * (wide % 2), 2 - high, 3 - 3 * high]
     middle = 3 - wide
     outer = (wide - 1) * 3
+    size = rows // PARTS
+    parts = range(PARTS)
+
+    load_image = pltpu.make_async_copy(image_hbm, image_raw, load_sem.at[0])
+    load_text = pltpu.make_async_copy(text_hbm, text_raw, load_sem.at[1])
+    load_pair = pltpu.make_async_copy(pair_hbm, pair_raw, load_sem.at[2])
+    load_image.start()
+    load_pair.start()
+    load_text.start()
 
     barrier = pltpu.get_barrier_semaphore()
 
@@ -121,47 +137,50 @@
     for step in range(1, 16):
         pl.semaphore_signal(barrier, inc=1, device_id=peer(step), device_id_type=MESH)
 
-    def block(place, column):
-        slot = place * 4 + column
-        return slot, gathered.at[pl.ds(pl.multiple_of(slot * rows, rows), rows), :]
-
-    image = image_ref[...].astype(jnp.float32)
+    def block(place, column, part):
+        slot = (place * 4 + column) * PARTS + part
+        return slot, gathered.at[pl.ds(pl.multiple_of(slot * size, size), size), :]
+
+    load_image.wait()
+    image = image_raw[...].astype(jnp.float32)
     image_inverse = lax.rsqrt(jnp.sum(image * image, axis=1, keepdims=True) + epsilon)
     gathered[pl.ds(pl.multiple_of(me * rows, rows), rows), :] = (image * image_inverse).astype(
         jnp.bfloat16
     )
-    own_pairs = jnp.concatenate([pair_ref[...], jnp.zeros((1, 128 - rows), jnp.int32)], axis=1)
-    pair_all[me] = own_pairs
+    load_pair.wait()
+    pair_all[me] = jnp.concatenate([pair_raw[...], jnp.zeros((1, 128 - rows), jnp.int32)], axis=1)
     pl.semaphore_wait(barrier, 15)
 
-    def send(number, place, column, to):
-        slot, view = block(place, column)
-        copy = pltpu.make_async_remote_copy(
+    def send(number, place, column, part, to):
+        slot, view = block(place, column, part)
+        pltpu.make_async_remote_copy(
             src_ref=view,
             dst_ref=view,
-            send_sem=send_sem.at[number],
+            send_sem=send_sem.at[number * PARTS + part],
             recv_sem=recv_sem.at[slot],
             device_id=to,
             device_id_type=MESH,
-        )
-        copy.start()
+        ).start()
 
     def sent(number):
-        view = gathered.at[pl.ds(0, rows), :]
-        pltpu.make_async_copy(view, view, send_sem.at[number]).wait()
-
-    def arrived(place, column):
-        slot, view = block(place, column)
+        view = gathered.at[pl.ds(0, size), :]
+        for part in parts:
+            pltpu.make_async_copy(view, view, send_sem.at[number * PARTS + part]).wait()
+
+    def arrived(place, column, part):
+        slot, view = block(place, column, part)
         pltpu.make_async_copy(view, view, recv_sem.at[slot]).wait()
 
-    send(0, wide, loop, {"wide": source[1], "loop": loop})
-
-    @pl.when(interior)
-    def _():
-        send(1, wide, loop, {"wide": middle, "loop": loop})
-
-    send(2, wide, loop, {"wide": wide, "loop": across})
-    send(3, wide, loop, {"wide": wide, "loop": sibling})
+    for part in parts:
+        send(0, wide, loop, part, {"wide": source[1], "loop": loop})
+
+        @pl.when(interior)
+        def _():
+            send(1, wide, loop, part, {"wide": middle, "loop": loop})
+
+        send(2, wide, loop, part, {"wide": wide, "loop": across})
+    for part in parts:
+        send(3, wide, loop, part, {"wide": wide, "loop": sibling})
     for step in range(1, 16):
         pltpu.make_async_remote_copy(
             src_ref=pair_all.at[me],
@@ -172,33 +191,38 @@
             device_id_type=MESH,
         ).start()
 
-    text = text_ref[...].astype(jnp.float32)
+    load_text.wait()
+    text = text_raw[...].astype(jnp.float32)
     inverse = lax.rsqrt(jnp.sum(text * text, axis=1, keepdims=True) + epsilon)
     text_bf[...] = (text * inverse).astype(jnp.bfloat16)
     scale_value = scale_ref[0]
     bias_value = bias_ref[0]
-    fifteen = pair_all.at[pl.ds(0, 15)]
-    pltpu.make_async_copy(fifteen, fifteen, small_recv.at[0]).wait()
-    for place in range(4):
-        pair_rows[place : place + 1, :] = jnp.concatenate(
-            [pair_all[place * 4 + column][:, :rows] for column in range(4)], axis=1
-        )
-
-    def pass_on(k):
-        arrived(source[k], loop)
+
+    def pass_on(k, part):
+        arrived(source[k], loop, part)
 
         @pl.when(interior)
         def _():
-            send(4 + k, source[k], loop, {"wide": middle if k == 1 else outer, "loop": loop})
-
-        send(8 + k, source[k], loop, {"wide": wide, "loop": across})
-        send(12 + k, source[k], loop, {"wide": wide, "loop": sibling})
-
-    def pass_across(k):
-        arrived(source[k], across)
-        send(16 + k, source[k], across, {"wide": wide, "loop": sibling})
-        arrived(source[k], sibling)
-        arrived(source[k], across_sibling)
+            send(
+                4 + k,
+                source[k],
+                loop,
+                part,
+                {"wide": middle if k == 1 else outer, "loop": loop},
+            )
+
+        send(8 + k, source[k], loop, part, {"wide": wide, "loop": across})
+        send(12 + k, source[k], loop, part, {"wide": wide, "loop": sibling})
+
+    def pass_across(k, part):
+        arrived(source[k], across, part)
+        send(16 + k, source[k], across, part, {"wide": wide, "loop": sibling})
+
+    def siblings(k):
+        for part in parts:
+            arrived(source[k], sibling, part)
+        for part in parts:
+            arrived(source[k], across_sibling, part)
 
     columns = me * rows + lax.broadcasted_iota(jnp.int32, (rows, 4 * rows), 0)
 
@@ -212,7 +236,10 @@
         positive = pair_rows[pl.ds(place, 1), :] == columns
         small = jnp.exp(-jnp.abs(logits))
         above = 1.0 + small
-        log_above = jnp.where(above == 1.0, small, jnp.log(above) * small / jnp.where(above == 1.0, 1.0, above - 1.0))
+        lost = above == 1.0
+        log_above = jnp.where(
+            lost, small, jnp.log(above) * small / jnp.where(lost, 1.0, above - 1.0)
+        )
         loss = log_above + jnp.maximum(jnp.where(positive, -logits, logits), 0.0)
         sigmoid = jnp.where(logits >= 0.0, 1.0, small) / above
         weights = (scale_value * (sigmoid - jnp.where(positive, 1.0, 0.0))).astype(jnp.bfloat16)
@@ -227,43 +254,59 @@
         else:
             total[...] += partial
 
-    pass_on(1)
-
-    @pl.when(interior)
-    def _():
-        pass_on(2)
-
-    pass_across(0)
+    for part in parts:
+        pass_on(1, part)
+
+        @pl.when(interior)
+        def _():
+            pass_on(2, part)
+
+        pass_across(0, part)
+    fifteen = pair_all.at[pl.ds(0, 15)]
+    pltpu.make_async_copy(fifteen, fifteen, small_recv.at[0]).wait()
+    for place in range(4):
+        pair_rows[place : place + 1, :] = jnp.concatenate(
+            [pair_all[place * 4 + column][:, :rows] for column in range(4)], axis=1
+        )
+    siblings(0)
     tile, weights, images = terms(0)
     accumulate(0, weights, images)
     loss_tile = tile
 
-    @pl.when(ends)
-    def _():
-        pass_on(2)
-
-    @pl.when(interior)
-    def _():
-        pass_on(3)
-
-    pass_across(1)
+    for part in parts:
+
+        @pl.when(ends)
+        def _():
+            pass_on(2, part)
+
+        @pl.when(interior)
+        def _():
+            pass_on(3, part)
+
+        pass_across(1, part)
+    siblings(1)
     tile, weights, images = terms(1)
     accumulate(1, weights, images)
     loss_tile += tile
 
-    @pl.when(ends)
-    def _():
-        pass_on(3)
-
-    pass_across(2)
+    for part in parts:
+
+        @pl.when(ends)
+        def _():
+            pass_on(3, part)
+
+        pass_across(2, part)
+    siblings(2)
     tile, weights, images = terms(2)
     accumulate(2, weights, images)
     loss_tile += tile
 
-    pass_across(3)
+    for part in parts:
+        pass_across(3, part)
+    siblings(3)
     tile, weights, images = terms(3)
     loss_tile += tile
-    loss_mine[...] = loss_tile
+    loss_mine[...] = jnp.sum(loss_tile, axis=0, keepdims=True)
     for step in range(1, 16):
         pltpu.make_async_remote_copy(
             src_ref=loss_mine,
@@ -274,7 +317,7 @@
             device_id_type=MESH,
         ).start()
     unit_grad = total[...] + jnp.dot(weights, images, preferred_element_type=jnp.float32)
-    text = text_ref[...].astype(jnp.float32)
+    text = text_raw[...].astype(jnp.float32)
     inverse = lax.rsqrt(jnp.sum(text * text, axis=1, keepdims=True) + epsilon)
     text_hat = text * inverse
     along = jnp.sum(text_hat * unit_grad, axis=1, keepdims=True)
@@ -299,29 +342,34 @@
     rows, width = text_embed.shape
     vmem = pl.BlockSpec(memory_space=pltpu.VMEM)
     smem = pl.BlockSpec(memory_space=pltpu.SMEM)
+    hbm = pl.BlockSpec(memory_space=pltpu.HBM)
     return pl.pallas_call(
         functools.partial(gather_kernel, rows),
         out_shape=(
             jax.ShapeDtypeStruct((rows, width), jnp.float32),
             jax.ShapeDtypeStruct((1,), jnp.float32),
         ),
-        in_specs=[vmem, vmem, vmem, smem, smem],
+        in_specs=[hbm, hbm, hbm, smem, smem],
         out_specs=(vmem, smem),
         scratch_shapes=[
             pltpu.VMEM((16 * rows, width), jnp.bfloat16),
+            pltpu.VMEM((rows, width), jnp.bfloat16),
+            pltpu.VMEM((rows, width), jnp.bfloat16),
+            pltpu.VMEM((1, rows), jnp.int32),
             pltpu.VMEM((16, 1, 128), jnp.int32),
             pltpu.VMEM((8, 4 * rows), jnp.int32),
-            pltpu.VMEM((15, 8, 128), jnp.float32),
-            pltpu.VMEM((8, 128), jnp.float32),
+            pltpu.VMEM((15, 1, 128), jnp.float32),
+            pltpu.VMEM((1, 128), jnp.float32),
             pltpu.VMEM((rows, width), jnp.bfloat16),
             pltpu.VMEM((rows, width), jnp.float32),
-            pltpu.SemaphoreType.DMA((20,)),
-            pltpu.SemaphoreType.DMA((16,)),
+            pltpu.SemaphoreType.DMA((3,)),
+            pltpu.SemaphoreType.DMA((20 * PARTS,)),
+            pltpu.SemaphoreType.DMA((16 * PARTS,)),
             pltpu.SemaphoreType.DMA((2,)),
             pltpu.SemaphoreType.DMA((2,)),
         ],
         compiler_params=pltpu.CompilerParams(
-            collective_id=0, has_side_effects=True, vmem_limit_bytes=32 * 1024 * 1024
+            collective_id=0, has_side_effects=True, vmem_limit_bytes=60 * 1024 * 1024
         ),
     )(image_embed, text_embed, pair_index.reshape(1, rows), logit_scale, logit_bias)
 

time: 38.2 us -> 34 us (0.89)
  Pallas kernels: 31.2 us -> 28.4 us
  local copies, waits for them, and re-layouts: 3.18 us -> 1.69 us
    pallas_call x1, Pallas kernels: 31.2 us -> 28.4 us  [gather_shards(): pl.pallas_call(functools.partial(gather_kernel, rows), out_shape=(jax.Sha...]
    unnamed x7 -> x1, local copies, waits for them, and re-layouts: 3.18 us -> 1.69 us
where the time goes in v2:
time: 34 us; the launch traced here: 33.8 us
  Pallas kernels  28.4 us (84%)
  between operations  3.75 us (11%)
  local copies, waits for them, and re-layouts  1.69 us (5%)
    pallas_call x1, Pallas kernels, gather_shards(): pl.pallas_call(functools.partial(gather_kernel, rows), out_shape=(jax.Sha...  28.4 us
    unnamed x1, local copies, waits for them, and re-layouts  1.69 us

profile of v2, /device:TPU:0, one launch (start us, length us, event | category | flops | bytes accessed | tf_op | source)
XLA Modules:
  0.0 33.8 jit_solution(1997656825587135933)
XLA Ops:
  1.9 28.4 %shard_map.68 = (f32[64,1152]{1,0:T(8,128)}, f32[1]{0:T(128)}) custom-call(bf16[64,1152]{1,0:T(8,128)(2,1)} %image_hbm.1, bf16[64,1152]{1,0:T(8,128)(2,1)} %text_hbm.1, s32[1,64]{1,0:T(1,128)} %bitcast.1, f32[1]{0:T(128)S(6)} %copy.9.scale_ref, f32[1]{0:T(128)S(6)} %copy.10.bias_ref), custom_call_target="tpu_custom_call" | custom-call | tf_op jit(solution)/shard_map/pallas_call | solution.py:346
  30.3 1.7 %copy.11 = f32[64,1152]{1,0:T(8,128)} copy(f32[64,1152]{1,0:T(8,128)} %get-tuple-element.4) | data formatting | bytes 589824

commit v3 on v2

--- a/solution.py
+++ b/solution.py
@@ -87,8 +87,8 @@
     image_hbm,
     text_hbm,
     pair_hbm,
-    scale_ref,
-    bias_ref,
+    scale_hbm,
+    bias_hbm,
     grad_ref,
     loss_ref,
     gathered,
@@ -101,6 +101,8 @@
     loss_mine,
     text_bf,
     total,
+    scale_ref,
+    bias_ref,
     load_sem,
     send_sem,
     recv_sem,
@@ -127,6 +129,10 @@
     load_image.start()
     load_pair.start()
     load_text.start()
+    load_scale = pltpu.make_async_copy(scale_hbm, scale_ref, load_sem.at[3])
+    load_bias = pltpu.make_async_copy(bias_hbm, bias_ref, load_sem.at[4])
+    load_scale.start()
+    load_bias.start()
 
     barrier = pltpu.get_barrier_semaphore()
 
@@ -172,13 +178,13 @@
         pltpu.make_async_copy(view, view, recv_sem.at[slot]).wait()
 
     for part in parts:
+        send(2, wide, loop, part, {"wide": wide, "loop": across})
         send(0, wide, loop, part, {"wide": source[1], "loop": loop})
 
         @pl.when(interior)
         def _():
             send(1, wide, loop, part, {"wide": middle, "loop": loop})
 
-        send(2, wide, loop, part, {"wide": wide, "loop": across})
     for part in parts:
         send(3, wide, loop, part, {"wide": wide, "loop": sibling})
     for step in range(1, 16):
@@ -195,6 +201,8 @@
     text = text_raw[...].astype(jnp.float32)
     inverse = lax.rsqrt(jnp.sum(text * text, axis=1, keepdims=True) + epsilon)
     text_bf[...] = (text * inverse).astype(jnp.bfloat16)
+    load_scale.wait()
+    load_bias.wait()
     scale_value = scale_ref[0]
     bias_value = bias_ref[0]
 
@@ -346,10 +354,10 @@
     return pl.pallas_call(
         functools.partial(gather_kernel, rows),
         out_shape=(
-            jax.ShapeDtypeStruct((rows, width), jnp.float32),
+            pltpu.VMEM((rows, width), jnp.float32),
             jax.ShapeDtypeStruct((1,), jnp.float32),
         ),
-        in_specs=[hbm, hbm, hbm, smem, smem],
+        in_specs=[hbm, hbm, hbm, hbm, hbm],
         out_specs=(vmem, smem),
         scratch_shapes=[
             pltpu.VMEM((16 * rows, width), jnp.bfloat16),
@@ -362,7 +370,9 @@
             pltpu.VMEM((1, 128), jnp.float32),
             pltpu.VMEM((rows, width), jnp.bfloat16),
             pltpu.VMEM((rows, width), jnp.float32),
-            pltpu.SemaphoreType.DMA((3,)),
+            pltpu.SMEM((1,), jnp.float32),
+            pltpu.SMEM((1,), jnp.float32),
+            pltpu.SemaphoreType.DMA((5,)),
             pltpu.SemaphoreType.DMA((20 * PARTS,)),
             pltpu.SemaphoreType.DMA((16 * PARTS,)),
             pltpu.SemaphoreType.DMA((2,)),

time: 34 us -> 32.8 us (0.965)
  local copies, waits for them, and re-layouts: 1.69 us -> 0.72 us
    unnamed x1, local copies, waits for them, and re-layouts: 1.69 us -> 0.72 us
where the time goes in v3:
time: 32.8 us; the launch traced here: 32.7 us
  Pallas kernels  28.3 us (86%)
  between operations  3.62 us (11%)
  local copies, waits for them, and re-layouts  0.72 us (2%)
    pallas_call x1, Pallas kernels, gather_shards(): pl.pallas_call(functools.partial(gather_kernel, rows), out_shape=(pltpu.V...  28.3 us
    unnamed x1, local copies, waits for them, and re-layouts  0.72 us

profile of v3, /device:TPU:0, one launch (start us, length us, event | category | flops | bytes accessed | tf_op | source)
XLA Modules:
  0.0 32.7 jit_solution(5485365836050045437)
XLA Ops:
  1.9 28.3 %shard_map.68 = (f32[64,1152]{1,0:T(8,128)S(1)}, f32[1]{0:T(128)}) custom-call(bf16[64,1152]{1,0:T(8,128)(2,1)} %image_hbm.1, bf16[64,1152]{1,0:T(8,128)(2,1)} %text_hbm.1, s32[1,64]{1,0:T(1,128)} %bitcast.1, f32[1]{0:T(128)S(6)} %copy.10.scale_hbm, f32[1]{0:T(128)S(6)} %copy.11.bias_hbm), custom_call_target="tpu_custom_call" | custom-call | tf_op jit(solution)/shard_map/pallas_call | solution.py:354
  30.2 0.7 %copy.9 = f32[64,1152]{1,0:T(8,128)} copy(f32[64,1152]{1,0:T(8,128)S(1)} %get-tuple-element.2) | data formatting | bytes 589824

commit v4 on v3

--- a/solution.py
+++ b/solution.py
@@ -226,22 +226,26 @@
         arrived(source[k], across, part)
         send(16 + k, source[k], across, part, {"wide": wide, "loop": sibling})
 
-    def siblings(k):
+    def siblings(k, column):
         for part in parts:
-            arrived(source[k], sibling, part)
-        for part in parts:
-            arrived(source[k], across_sibling, part)
-
-    columns = me * rows + lax.broadcasted_iota(jnp.int32, (rows, 4 * rows), 0)
-
-    def terms(k):
+            arrived(source[k], column, part)
+
+    lanes = 2 * rows
+
+    def terms(k, column=None):
         place = source[k]
-        images = gathered[pl.ds(pl.multiple_of(place * 4 * rows, 4 * rows), 4 * rows), :]
+        if column is None:
+            first, count = place * 2, 2
+        else:
+            first, count = place * 2 + column // 2, 1
+        images = gathered[pl.ds(pl.multiple_of(first * lanes, lanes), count * lanes), :]
         scores = lax.dot_general(
             text_bf[...], images, (((1,), (1,)), ((), ())), preferred_element_type=jnp.float32
         )
         logits = scale_value * scores + bias_value
-        positive = pair_rows[pl.ds(place, 1), :] == columns
+        columns = me * rows + lax.broadcasted_iota(jnp.int32, logits.shape, 0)
+        held = [pair_rows[pl.ds(first + i, 1), :] for i in range(count)]
+        positive = (held[0] if count == 1 else jnp.concatenate(held, axis=1)) == columns
         small = jnp.exp(-jnp.abs(logits))
         above = 1.0 + small
         lost = above == 1.0
@@ -251,16 +255,12 @@
         loss = log_above + jnp.maximum(jnp.where(positive, -logits, logits), 0.0)
         sigmoid = jnp.where(logits >= 0.0, 1.0, small) / above
         weights = (scale_value * (sigmoid - jnp.where(positive, 1.0, 0.0))).astype(jnp.bfloat16)
-        tile = loss[:, :128] + loss[:, 128:]
-        tile = jnp.sum(tile.reshape(rows // 8, 8, 128), axis=0)
+        tile = loss if count == 1 else loss[:, :lanes] + loss[:, lanes:]
+        tile = jnp.sum(tile.reshape(rows // 8, 8, lanes), axis=0)
         return tile, weights, images
 
-    def accumulate(k, weights, images):
-        partial = jnp.dot(weights, images, preferred_element_type=jnp.float32)
-        if k == 0:
-            total[...] = partial
-        else:
-            total[...] += partial
+    def accumulate(weights, images):
+        total[...] += jnp.dot(weights, images, preferred_element_type=jnp.float32)
 
     for part in parts:
         pass_on(1, part)
@@ -272,14 +272,14 @@
         pass_across(0, part)
     fifteen = pair_all.at[pl.ds(0, 15)]
     pltpu.make_async_copy(fifteen, fifteen, small_recv.at[0]).wait()
-    for place in range(4):
-        pair_rows[place : place + 1, :] = jnp.concatenate(
-            [pair_all[place * 4 + column][:, :rows] for column in range(4)], axis=1
+    for chip in range(8):
+        pair_rows[chip : chip + 1, :] = jnp.concatenate(
+            [pair_all[chip * 2 + core][:, :rows] for core in range(2)], axis=1
         )
-    siblings(0)
-    tile, weights, images = terms(0)
-    accumulate(0, weights, images)
-    loss_tile = tile
+    siblings(0, sibling)
+    siblings(0, across_sibling)
+    loss_tile, weights, images = terms(0)
+    total[...] = jnp.dot(weights, images, preferred_element_type=jnp.float32)
 
     for part in parts:
 
@@ -292,9 +292,9 @@
             pass_on(3, part)
 
         pass_across(1, part)
-    siblings(1)
-    tile, weights, images = terms(1)
-    accumulate(1, weights, images)
+    siblings(1, sibling)
+    tile, weights, images = terms(1, loop)
+    accumulate(weights, images)
     loss_tile += tile
 
     for part in parts:
@@ -304,15 +304,24 @@
             pass_on(3, part)
 
         pass_across(2, part)
-    siblings(2)
+    siblings(2, sibling)
+    siblings(2, across_sibling)
     tile, weights, images = terms(2)
-    accumulate(2, weights, images)
+    accumulate(weights, images)
     loss_tile += tile
+    siblings(3, sibling)
+    tile, weights, images = terms(3, loop)
+    accumulate(weights, images)
+    loss_tile += tile
 
     for part in parts:
         pass_across(3, part)
-    siblings(3)
-    tile, weights, images = terms(3)
+    siblings(1, across_sibling)
+    tile, weights, images = terms(1, across)
+    accumulate(weights, images)
+    loss_tile += tile
+    siblings(3, across_sibling)
+    tile, weights, images = terms(3, across)
     loss_tile += tile
     loss_mine[...] = jnp.sum(loss_tile, axis=0, keepdims=True)
     for step in range(1, 16):
@@ -365,7 +374,7 @@
             pltpu.VMEM((rows, width), jnp.bfloat16),
             pltpu.VMEM((1, rows), jnp.int32),
             pltpu.VMEM((16, 1, 128), jnp.int32),
-            pltpu.VMEM((8, 4 * rows), jnp.int32),
+            pltpu.VMEM((8, 2 * rows), jnp.int32),
             pltpu.VMEM((15, 1, 128), jnp.float32),
             pltpu.VMEM((1, 128), jnp.float32),
             pltpu.VMEM((rows, width), jnp.bfloat16),

time: 32.8 us -> 32.7 us (level)
  no operation moved by 1% of the time
where the time goes in v4:
time: 32.7 us; the launch traced here: 32.5 us
  Pallas kernels  28.1 us (86%)
  between operations  3.62 us (11%)
  local copies, waits for them, and re-layouts  0.72 us (2%)
    pallas_call x1, Pallas kernels, gather_shards(): pl.pallas_call(functools.partial(gather_kernel, rows), out_shape=(pltpu.V...  28.1 us
    unnamed x1, local copies, waits for them, and re-layouts  0.72 us

profile of v4, /device:TPU:0, one launch (start us, length us, event | category | flops | bytes accessed | tf_op | source)
XLA Modules:
  0.0 32.5 jit_solution(2210267561426262889)
XLA Ops:
  1.9 28.1 %shard_map.68 = (f32[64,1152]{1,0:T(8,128)S(1)}, f32[1]{0:T(128)}) custom-call(bf16[64,1152]{1,0:T(8,128)(2,1)} %image_hbm.1, bf16[64,1152]{1,0:T(8,128)(2,1)} %text_hbm.1, s32[1,64]{1,0:T(1,128)} %bitcast.1, f32[1]{0:T(128)S(6)} %copy.10.scale_hbm, f32[1]{0:T(128)S(6)} %copy.11.bias_hbm), custom_call_target="tpu_custom_call" | custom-call | tf_op jit(solution)/shard_map/pallas_call | solution.py:363
  30.1 0.7 %copy.9 = f32[64,1152]{1,0:T(8,128)} copy(f32[64,1152]{1,0:T(8,128)S(1)} %get-tuple-element.2) | data formatting | bytes 589824
